TPU v7x, 32 devices: a whole 2x2x4 slice. The times are simulated.
32 devices in a mesh: level: 4 (over z), leaf: 4 (over x, core), rhs: 2 (over y).
Axes of the slice: x: 2, y: 2, z: 4, core: 2. Of those that a mesh axis runs over, the one named last changes fastest.
Arguments:
- charges: float32 [64, 65536], P(None, ('level', 'leaf', 'rhs')), may hold values from -6 to 6
- cluster_order: int32 [65536], P(('level', 'leaf')), may hold values from 0 to 4095, as said below
- near_tiles: float32 [512, 4, 128, 128], P(('level', 'leaf', 'rhs')), may hold values from -0.25 to 0.25
- near_index: int32 [512, 4], P(('level', 'leaf', 'rhs')), may hold values from 0 to 31, as said below
- near_count: int32 [512], P(('level', 'leaf', 'rhs')), may hold values from 1 to 4, as said below
- proj_basis: float32 [4, 65536, 256], P(None, ('level', 'leaf', 'rhs'))
- corr_basis: float32 [4, 256, 65536], P(None, None, ('level', 'leaf', 'rhs')), may hold values from -0.1875 to 0.1875
- coupling: float32 [16, 4, 2, 256, 256], P(('level', 'leaf'))
Outputs:
- solution: float32 [64, 65536], P(None, ('level', 'leaf', 'rhs'))
Inputs may be any that keep to these rules, and one draw needn't show every extreme that they name: `cluster_order`: every aligned block of 4096 entries is a permutation of 0 to 4095. `near_index`: the entries of a row are distinct tile numbers of the same leaf, the first being the row's own tile. `near_count`: the first tile row of every leaf has 4.
All inputs are finite; a program needn't handle non-finite values.
Results may differ from a plain program's by a relative error of at most 0.0001.
Values sent between devices are 32-bit elements; how exact they have to be, the bound alone decides.
A program may use at most 128 MiB of HBM per device.

v0:
```python
import jax
import jax.numpy as jnp
from jax import lax
from jax.sharding import PartitionSpec as P


def from_partner(block, axis, distance):
    count = lax.axis_size(axis)
    route = []
    for low in range(count):
        high = low | 1 << distance
        if high != low and high < count:
            route += [(low, high), (high, low)]
    return lax.ppermute(block, axis, route)


def partner_sum(values, bit_pos):
    return from_partner(values, ("level", "leaf"), bit_pos)


def local(
    charges, cluster_order, near_tiles, near_index, near_count, proj_basis, corr_basis, coupling
):
    rhs_count = charges.shape[0]
    row_count = charges.shape[1]
    near_slots = near_tiles.shape[1]
    tile_size = near_tiles.shape[2]
    leaf_charges = lax.all_gather(charges, "rhs", axis=1, tiled=True)
    ordered = jnp.take(leaf_charges, cluster_order, axis=1)
    blocks = ordered.reshape(rhs_count, -1, tile_size)
    picked = blocks[:, near_index]
    live_mask = (jnp.arange(near_slots)[None, :] < near_count[:, None]).astype(jnp.float32)
    picked = picked * live_mask[None, :, :, None]
    current = jnp.einsum("rtki,tkio->rto", picked, near_tiles, precision=lax.Precision.HIGHEST)
    current = current.reshape(rhs_count, row_count)
    for height in range(proj_basis.shape[0]):
        projected = jnp.dot(
            current,
            proj_basis[height],
            precision=lax.Precision.HIGHEST,
            preferred_element_type=jnp.float32,
        )
        own_sum = lax.psum(projected, "rhs")
        for bit_pos in range(height):
            own_sum = own_sum + partner_sum(own_sum, bit_pos)
        sib_sum = partner_sum(own_sum, height)
        coeff = jnp.dot(
            own_sum,
            coupling[0, height, 0],
            precision=lax.Precision.HIGHEST,
            preferred_element_type=jnp.float32,
        )
        coeff = coeff + jnp.dot(
            sib_sum,
            coupling[0, height, 1],
            precision=lax.Precision.HIGHEST,
            preferred_element_type=jnp.float32,
        )
        current = current - jnp.dot(
            coeff,
            corr_basis[height],
            precision=lax.Precision.HIGHEST,
            preferred_element_type=jnp.float32,
        )
    return current


def solution(mesh):
    return jax.shard_map(
        local,
        mesh=mesh,
        in_specs=(
            P(None, ("level", "leaf", "rhs")),
            P(("level", "leaf")),
            P(("level", "leaf", "rhs"), None, None, None),
            P(("level", "leaf", "rhs"), None),
            P(("level", "leaf", "rhs")),
            P(None, ("level", "leaf", "rhs"), None),
            P(None, None, ("level", "leaf", "rhs")),
            P(("level", "leaf"), None, None, None, None),
        ),
        out_specs=P(None, ("level", "leaf", "rhs")),
        check_vma=False,
    )
```

profile of v0, /device:TPU:0, one launch (start us, length us, event | category | flops | bytes accessed | tf_op | source)
XLA Modules:
  0.0 227.6 jit_solution(4937294131760515816)
XLA Ops:
  9.3 35.6 %all-gather.2.cloned.1.call-done = f32[64,4096]{0,1:T(8,128)} async-done(((f32[64,2048]{0,1:T(8,128)}), f32[64,4096]{0,1:T(8,128)}) %all-gather.2.cloned.1.call-update) | async-done | bytes 1048592 | tf_op jit(solution)/shard_map/all_gather | solution.py:28
  44.9 15.7 %gather_fusion = f32[4096,64]{1,0:T(8,128)} fusion(f32[64,4096]{0,1:T(8,128)} %all-gather.2.cloned.1.call-done, s32[4096]{0:T(1024)S(1)} %fusion.49), kind=kCustom, calls=%fused_computation | custom fusion | bytes 2113536 | tf_op jit(solution)/shard_map/jit(_take)/gather | solution.py:29
  62.6 2.8 %gather_fusion.1 = f32[64,64,128]{1,2,0:T(8,128)} fusion(f32[64,32,128]{0,2,1:T(8,128)S(1)} %broadcast_select_fusion, s32[1024]{0:T(1024)S(1)} %pad_clamp_fusion), kind=kCustom, calls=%fused_computation.1 | custom fusion | bytes 4194560 | tf_op jit(solution)/shard_map/gather | solution.py:31
  65.3 2.8 %copy.14 = f32[64,64,128]{2,1,0:T(8,128)S(1)} copy(f32[64,64,128]{1,2,0:T(8,128)} %gather_fusion.1) | data formatting | bytes 4194304 | tf_op jit(solution)/shard_map/gather | solution.py:31
  68.2 4.6 %fusion.23 = f32[16,8,8,128]{3,2,1,0:T(8,128)S(1)} fusion(f32[16,4,128,128]{3,2,1,0:T(8,128)} %param.10, f32[16,4,64,128]{3,2,1,0:T(8,128)S(1)} %bitcast.85, f32[16,4]{1,0:T(8,128)S(1)} %fusion.50), kind=kOutput, calls=%fused_computation.29 | convolution fusion | flops 805830656 | bytes 6816000 | tf_op jit(solution)/shard_map/rtki,tkio->rto/dot_general | solution.py:34
  72.8 3.4 %fusion.10 = f32[64,256]{1,0:T(8,128)} fusion(f32[4,2048,256]{2,1,0:T(8,128)} %param.13, f32[16,8,8,128]{3,2,1,0:T(8,128)S(1)} %fusion.23), kind=kOutput, calls=%fused_computation.16 | convolution fusion | flops 402653184 | bytes 2686976 | tf_op jit(solution)/shard_map/dot_general | solution.py:37
  76.3 20.9 %all-reduce.5.cloned.1.call-done = f32[64,256]{1,0:T(8,128)} async-done(((f32[64,256]{1,0:T(8,128)}), f32[64,256]{1,0:T(8,128)}) %all-reduce.5.cloned.1.call-update) | async-done | bytes 65552 | tf_op jit(solution)/shard_map/psum | solution.py:43
  99.8 3.0 %convolution_subtract_fusion.3 = f32[64,2048]{1,0:T(8,128)S(1)} fusion(f32[64,256]{1,0:T(8,128)S(1)} %convolution_add_fusion.3, f32[4,256,2048]{2,1,0:T(8,128)} %param.14, f32[16,8,8,128]{3,2,1,0:T(8,128)S(1)} %fusion.23), kind=kOutput, calls=%fused_computation.5 | convolution fusion | flops 402784256 | bytes 3211264 | tf_op jit(solution)/shard_map/dot_general | solution.py:59
  102.8 3.5 %fusion.7 = f32[64,256]{1,0:T(8,128)} fusion(f32[64,2048]{1,0:T(8,128)S(1)} %convolution_subtract_fusion.3, f32[4,2048,256]{2,1,0:T(8,128)} %param.13), kind=kOutput, calls=%fused_computation.13 | convolution fusion | flops 402653184 | bytes 2686976 | tf_op jit(solution)/shard_map/dot_general | solution.py:37
  106.4 20.9 %all-reduce.7.cloned.1.call-done = f32[64,256]{1,0:T(8,128)} async-done(((f32[64,256]{1,0:T(8,128)}), f32[64,256]{1,0:T(8,128)}) %all-reduce.7.cloned.1.call-update) | async-done | bytes 65552 | tf_op jit(solution)/shard_map/psum | solution.py:43
  131.1 2.8 %collective-permute-done.2 = f32[64,256]{1,0:T(8,128)S(1)} collective-permute-done((f32[64,256]{1,0:T(8,128)S(1)}, f32[64,256]{1,0:T(8,128)S(1)}, u32[]{:S(2)}, u32[]{:S(2)}) %collective-permute-start.2) | collective-permute-done | bytes 65568 | tf_op jit(solution)/shard_map/ppermute | solution.py:14
  134.4 3.0 %convolution_subtract_fusion.2 = f32[64,2048]{1,0:T(8,128)S(1)} fusion(f32[64,2048]{1,0:T(8,128)S(1)} %convolution_subtract_fusion.3, f32[64,256]{1,0:T(8,128)S(1)} %convolution_add_fusion.2, f32[4,256,2048]{2,1,0:T(8,128)} %param.14), kind=kOutput, calls=%fused_computation.4 | convolution fusion | flops 402784256 | bytes 3211264 | tf_op jit(solution)/shard_map/dot_general | solution.py:59
  137.4 3.4 %fusion.4 = f32[64,256]{1,0:T(8,128)} fusion(f32[64,2048]{1,0:T(8,128)S(1)} %convolution_subtract_fusion.2, f32[4,2048,256]{2,1,0:T(8,128)} %param.13), kind=kOutput, calls=%fused_computation.10 | convolution fusion | flops 402653184 | bytes 2686976 | tf_op jit(solution)/shard_map/dot_general | solution.py:37
  141.1 20.7 %all-reduce.9.cloned.1.call-done = f32[64,256]{1,0:T(8,128)} async-done(((f32[64,256]{1,0:T(8,128)}), f32[64,256]{1,0:T(8,128)}) %all-reduce.9.cloned.1.call-update) | async-done | bytes 65552 | tf_op jit(solution)/shard_map/psum | solution.py:43
  165.6 2.8 %collective-permute-done.4 = f32[64,256]{1,0:T(8,128)S(1)} collective-permute-done((f32[64,256]{1,0:T(8,128)S(1)}, f32[64,256]{1,0:T(8,128)S(1)}, u32[]{:S(2)}, u32[]{:S(2)}) %collective-permute-start.4) | collective-permute-done | bytes 65568 | tf_op jit(solution)/shard_map/ppermute | solution.py:14
  170.0 2.8 %collective-permute-done.5 = f32[64,256]{1,0:T(8,128)S(1)} collective-permute-done((f32[64,256]{1,0:T(8,128)S(1)}, f32[64,256]{1,0:T(8,128)S(1)}, u32[]{:S(2)}, u32[]{:S(2)}) %collective-permute-start.5) | collective-permute-done | bytes 65568 | tf_op jit(solution)/shard_map/ppermute | solution.py:14
  173.3 3.0 %convolution_subtract_fusion.1 = f32[64,2048]{1,0:T(8,128)S(1)} fusion(f32[64,2048]{1,0:T(8,128)S(1)} %convolution_subtract_fusion.2, f32[64,256]{1,0:T(8,128)S(1)} %convolution_add_fusion.1, f32[4,256,2048]{2,1,0:T(8,128)} %param.14), kind=kOutput, calls=%fused_computation.3 | convolution fusion | flops 402784256 | bytes 3211264 | tf_op jit(solution)/shard_map/dot_general | solution.py:59
  176.2 3.4 %fusion.1 = f32[64,256]{1,0:T(8,128)} fusion(f32[64,2048]{1,0:T(8,128)S(1)} %convolution_subtract_fusion.1, f32[4,2048,256]{2,1,0:T(8,128)} %param.13), kind=kOutput, calls=%fused_computation.7 | convolution fusion | flops 402653184 | bytes 2686976 | tf_op jit(solution)/shard_map/dot_general | solution.py:37
  179.7 20.9 %all-reduce.11.cloned.1.call-done = f32[64,256]{1,0:T(8,128)} async-done(((f32[64,256]{1,0:T(8,128)}), f32[64,256]{1,0:T(8,128)}) %all-reduce.11.cloned.1.call-update) | async-done | bytes 65552 | tf_op jit(solution)/shard_map/psum | solution.py:43
  204.4 2.8 %collective-permute-done.7 = f32[64,256]{1,0:T(8,128)S(1)} collective-permute-done((f32[64,256]{1,0:T(8,128)S(1)}, f32[64,256]{1,0:T(8,128)S(1)}, u32[]{:S(2)}, u32[]{:S(2)}) %collective-permute-start.7) | collective-permute-done | bytes 65568 | tf_op jit(solution)/shard_map/ppermute | solution.py:14
  208.8 2.8 %collective-permute-done.8 = f32[64,256]{1,0:T(8,128)S(1)} collective-permute-done((f32[64,256]{1,0:T(8,128)S(1)}, f32[64,256]{1,0:T(8,128)S(1)}, u32[]{:S(2)}, u32[]{:S(2)}) %collective-permute-start.8) | collective-permute-done | bytes 65568 | tf_op jit(solution)/shard_map/ppermute | solution.py:14
  211.6 2.5 %collective-permute-start.9 = (f32[64,256]{1,0:T(8,128)S(1)}, f32[64,256]{1,0:T(8,128)S(1)}, u32[]{:S(2)}, u32[]{:S(2)}) collective-permute-start(f32[64,256]{1,0:T(8,128)S(1)} %add.64), channel_id=1, source_target_pairs={{0,16},{16,0},{2,18},{18,2},{4,20},{20,4},{6,22},{22,6},{8,24},{24... | collective-permute-start | bytes 196616 | tf_op jit(solution)/shard_map/ppermute | solution.py:14
  214.1 2.8 %collective-permute-done.9 = f32[64,256]{1,0:T(8,128)S(1)} collective-permute-done((f32[64,256]{1,0:T(8,128)S(1)}, f32[64,256]{1,0:T(8,128)S(1)}, u32[]{:S(2)}, u32[]{:S(2)}) %collective-permute-start.9) | collective-permute-done | bytes 65568 | tf_op jit(solution)/shard_map/ppermute | solution.py:14
  217.3 3.8 %convolution_subtract_fusion = f32[64,2048]{1,0:T(8,128)} fusion(f32[64,2048]{1,0:T(8,128)S(1)} %convolution_subtract_fusion.1, f32[64,256]{1,0:T(8,128)S(1)} %convolution_add_fusion, f32[4,256,2048]{2,1,0:T(8,128)} %param.14), kind=kOutput, calls=%fused_computation.2 | convolution fusion | flops 402784256 | bytes 3211264 | tf_op jit(solution)/shard_map/dot_general | solution.py:59
  (54 shorter events, 23.8 us)
Async XLA Ops:
  6.5 2.5 %copy-start.2 = (s32[16,4]{0,1:T(4,128)S(1)}, s32[16,4]{0,1:T(4,128)}, u32[]{:S(2)}) copy-start(s32[16,4]{0,1:T(4,128)} %param.11) | copy-start | bytes 772
  6.5 2.7 %copy-start.3 = (s32[16]{0:T(128)S(1)}, s32[16]{0:T(128)}, u32[]{:S(2)}) copy-start(s32[16]{0:T(128)} %param.12) | copy-start | bytes 196
  6.5 2.8 %copy-start.1 = (s32[4096]{0:T(1024)S(1)}, s32[4096]{0:T(1024)}, u32[]{:S(2)}) copy-start(s32[4096]{0:T(1024)} %param.9) | copy-start | bytes 49156
  6.5 38.4 %all-gather.2.cloned.1.call-start = ((), (), s32[]{:S(2)}) async-start(), calls=%async_computation | async-start | bytes 3145728 | tf_op jit(solution)/shard_map/all_gather | solution.py:28
  8.9 88.2 %all-reduce.5.cloned.1.call-start = ((), (), s32[]{:S(2)}) async-start(), calls=%async_computation.1 | async-start | bytes 131072 | tf_op jit(solution)/shard_map/psum | solution.py:43
  76.2 51.1 %all-reduce.7.cloned.1.call-start = ((), (), s32[]{:S(2)}) async-start(), calls=%async_computation.2 | async-start | bytes 131072 | tf_op jit(solution)/shard_map/psum | solution.py:43
  97.1 1.5 collective-permute-start
  102.8 31.2 %copy-start = (f32[1,4,2,256,256]{4,3,2,1,0:T(8,128)S(1)}, f32[1,4,2,256,256]{4,3,2,1,0:T(8,128)}, u32[]{:S(2)}) copy-start(f32[1,4,2,256,256]{4,3,2,1,0:T(8,128)} %param.15) | copy-start | bytes 6291460
  106.3 55.4 %all-reduce.9.cloned.1.call-start = ((), (), s32[]{:S(2)}) async-start(), calls=%async_computation.3 | async-start | bytes 131072 | tf_op jit(solution)/shard_map/psum | solution.py:43
  127.3 1.5 collective-permute-start.1
  129.6 4.3 %collective-permute-start.2 = (f32[64,256]{1,0:T(8,128)S(1)}, f32[64,256]{1,0:T(8,128)S(1)}, u32[]{:S(2)}, u32[]{:S(2)}) collective-permute-start(f32[64,256]{1,0:T(8,128)S(1)} %add.57), channel_id=1, source_target_pairs={{0,4},{4,0},{2,6},{6,2},{8,12},{12,8},{10,14},{14,10},{16,20},{20,... | collective-permute-start | bytes 196616 | tf_op jit(solution)/shard_map/ppermute | solution.py:14
  140.8 59.8 %all-reduce.11.cloned.1.call-start = ((), (), s32[]{:S(2)}) async-start(), calls=%async_computation.4 | async-start | bytes 131072 | tf_op jit(solution)/shard_map/psum | solution.py:43
  161.8 1.5 collective-permute-start.3
  164.1 4.3 %collective-permute-start.4 = (f32[64,256]{1,0:T(8,128)S(1)}, f32[64,256]{1,0:T(8,128)S(1)}, u32[]{:S(2)}, u32[]{:S(2)}) collective-permute-start(f32[64,256]{1,0:T(8,128)S(1)} %add.59), channel_id=1, source_target_pairs={{0,4},{4,0},{2,6},{6,2},{8,12},{12,8},{10,14},{14,10},{16,20},{20,... | collective-permute-start | bytes 196616 | tf_op jit(solution)/shard_map/ppermute | solution.py:14
  168.4 4.3 %collective-permute-start.5 = (f32[64,256]{1,0:T(8,128)S(1)}, f32[64,256]{1,0:T(8,128)S(1)}, u32[]{:S(2)}, u32[]{:S(2)}) collective-permute-start(f32[64,256]{1,0:T(8,128)S(1)} %add.60), channel_id=1, source_target_pairs={{0,8},{8,0},{2,10},{10,2},{4,12},{12,4},{6,14},{14,6},{16,24},{24,... | collective-permute-start | bytes 196616 | tf_op jit(solution)/shard_map/ppermute | solution.py:14
  200.6 1.5 collective-permute-start.6
  202.9 4.3 %collective-permute-start.7 = (f32[64,256]{1,0:T(8,128)S(1)}, f32[64,256]{1,0:T(8,128)S(1)}, u32[]{:S(2)}, u32[]{:S(2)}) collective-permute-start(f32[64,256]{1,0:T(8,128)S(1)} %add.62), channel_id=1, source_target_pairs={{0,4},{4,0},{2,6},{6,2},{8,12},{12,8},{10,14},{14,10},{16,20},{20,... | collective-permute-start | bytes 196616 | tf_op jit(solution)/shard_map/ppermute | solution.py:14
  207.3 4.3 %collective-permute-start.8 = (f32[64,256]{1,0:T(8,128)S(1)}, f32[64,256]{1,0:T(8,128)S(1)}, u32[]{:S(2)}, u32[]{:S(2)}) collective-permute-start(f32[64,256]{1,0:T(8,128)S(1)} %add.63), channel_id=1, source_target_pairs={{0,8},{8,0},{2,10},{10,2},{4,12},{12,4},{6,14},{14,6},{16,24},{24,... | collective-permute-start | bytes 196616 | tf_op jit(solution)/shard_map/ppermute | solution.py:14
  211.6 5.2 %collective-permute-start.9 = (f32[64,256]{1,0:T(8,128)S(1)}, f32[64,256]{1,0:T(8,128)S(1)}, u32[]{:S(2)}, u32[]{:S(2)}) collective-permute-start(f32[64,256]{1,0:T(8,128)S(1)} %add.64), channel_id=1, source_target_pairs={{0,16},{16,0},{2,18},{18,2},{4,20},{20,4},{6,22},{22,6},{8,24},{24... | collective-permute-start | bytes 196616 | tf_op jit(solution)/shard_map/ppermute | solution.py:14
Sparse Core Ops, SparseCore 0:
  9.1 35.8 all-gather.1
  76.3 20.7 all-reduce.4
  106.5 20.7 all-reduce.6
  141.0 20.7 all-reduce.8
  179.8 20.7 all-reduce.10
where the time goes:
time: 228 us
  waiting for transfers between devices  140 us (61%)
  matrix products  34.9 us (15%)
  local copies, waits for them, and re-layouts  23.9 us (10%)
  between operations  13.3 us (6%)
  starting transfers between devices  10.5 us (5%)
  other arithmetic  4.61 us (2%)
    psum x4, waiting for transfers between devices, local(): own_sum = lax.psum(projected, 'rhs')  83.4 us
    all_gather x1, waiting for transfers between devices, local(): leaf_charges = lax.all_gather(charges, 'rhs', axis=1, tiled=True)  35.6 us
    ppermute x10, waiting for transfers between devices, from_partner(): return lax.ppermute(block, axis, route)  21.3 us
    gather x1, local copies, waits for them, and re-layouts, local(): ordered = jnp.take(leaf_charges, cluster_order, axis=1)  15.7 us
    dot_general x4, matrix products, local(): jnp.dot(current, proj_basis[height], precision=lax.Precision.HIGHEST, pre...  13.7 us
    dot_general x4, matrix products, local(): jnp.dot(coeff, corr_basis[height], precision=lax.Precision.HIGHEST, prefe...  12.7 us
    ppermute x10, starting transfers between devices, from_partner(): return lax.ppermute(block, axis, route)  10.2 us
    gather x2, local copies, waits for them, and re-layouts, local(): picked = blocks[:, near_index]  5.6 us
  transfers between devices with their start and end apart: 15, of which 15 were waited for; matrix products, arithmetic and copies ran while one was open for 1% of the time, Pallas kernels for 0%

commit v1 on v0

v1 whole, which is shorter than its diff:
```python
import jax
import jax.numpy as jnp
from jax import lax
from jax.experimental import pallas as pl
from jax.experimental.pallas import tpu as pltpu
from jax.sharding import PartitionSpec as P

F32 = jnp.float32
BF16 = jnp.bfloat16
MESH = pl.DeviceIdType.MESH
POS = 512
SRC = 512
SUB = 256


def flip(index, bit):
    return index + bit - 2 * bit * ((index // bit) % 2)


def split(values):
    high = values.astype(BF16)
    low = (values - high.astype(F32)).astype(BF16)
    return high, low


def stacked(values):
    return jnp.concatenate(split(values), axis=0)


def dot(left, right):
    return jnp.dot(left, right, preferred_element_type=F32)


def dot3(left_hl, right_high, right_low):
    rows = left_hl.shape[0] // 2
    both = dot(left_hl, right_high)
    return both[:rows] + both[rows:] + dot(left_hl[:rows], right_low)


def kernel(
    near_index, near_count, order, charges, near, proj, corr, coup, out,
    mine, other, acc, ordered, near_f, near_hl, proj_f, proj_h, proj_l, corr_f, corr_h, corr_l,
    coup_f, coup_h, coup_l, current, part, rs0, stage0, ag0, rs, stage, ag, zsend, zrecv,
    load_sem, ex_send, ex_recv, rs_send, rs_recv, ag_send, ag_recv, z_send, z_recv,
):
    heights = proj.shape[0]
    rhs_count, half = charges.shape
    level, leaf, side = lax.axis_index("level"), lax.axis_index("leaf"), lax.axis_index("rhs")
    core, column = leaf % 2, leaf // 2
    rank = side + 2 * core + 4 * column
    rank0 = side + 2 * core

    def rank_of(rel):
        number = rank
        for bit in (1, 2, 4):
            if rel & bit:
                number = flip(number, bit)
        return number

    def plane(rel):
        where, there = leaf, side
        if rel & 1:
            there = 1 - side
        if rel & 2:
            where = flip(where, 1)
        if rel & 4:
            where = flip(where, 2)
        return {"level": level, "leaf": where, "rhs": there}

    def column_of(rel):
        number = level
        for bit in (1, 2):
            if rel & bit:
                number = flip(number, bit)
        return {"level": number, "leaf": leaf, "rhs": side}

    loads = [pltpu.make_async_copy(charges, mine, load_sem.at[0])]
    for height in range(heights):
        loads.append(pltpu.make_async_copy(proj.at[height], proj_f.at[height], load_sem.at[1 + 2 * height]))
        loads.append(pltpu.make_async_copy(corr.at[height], corr_f.at[height], load_sem.at[2 + 2 * height]))
    loads.append(pltpu.make_async_copy(near, near_f, load_sem.at[1 + 2 * heights]))
    loads.append(pltpu.make_async_copy(coup, coup_f, load_sem.at[2 + 2 * heights]))
    for load in loads:
        load.start()

    barrier = pltpu.get_barrier_semaphore()
    for rel in range(1, 8):
        pl.semaphore_signal(barrier, inc=1, device_id=plane(rel), device_id_type=MESH)
    for rel in range(1, 4):
        pl.semaphore_signal(barrier, inc=1, device_id=column_of(rel), device_id_type=MESH)
    pl.semaphore_wait(barrier, 10)

    sends = []

    def send(src, dst, send_sem, recv_sem, device):
        copy = pltpu.make_async_remote_copy(
            src_ref=src, dst_ref=dst, send_sem=send_sem, recv_sem=recv_sem,
            device_id=device, device_id_type=MESH,
        )
        copy.start()
        sends.append(copy)
        return copy

    chunks = half // SRC
    arrivals = []
    for chunk in range(chunks):
        cols = pl.ds(chunk * SRC, SRC)
        arrivals.append(send(
            charges.at[:, cols], other.at[:, cols], ex_send.at[chunk], ex_recv.at[chunk], plane(1)
        ))

    rows_of = lax.broadcasted_iota(jnp.int32, (SUB, POS), 0)

    def place(source, first, start, fresh):
        parts = stacked(source[:, pl.ds(start, SRC)])

        def body(step, carry):
            wanted = order[step]
            masks = []
            for sub in range(SRC // SUB):
                rel = wanted - (first + start + sub * SUB)
                masks.append(jnp.where(rows_of == rel, 1.0, 0.0).astype(BF16))
            got = dot(parts, jnp.concatenate(masks, axis=0))
            if fresh:
                acc[step] = got
            else:
                acc[step] = acc[step] + got
            return carry

        lax.fori_loop(0, order.shape[0], body, 0)

    loads[0].wait()
    for chunk in range(chunks):
        place(mine, side * half, chunk * SRC, chunk == 0)

    for height in range(heights):
        loads[1 + 2 * height].wait()
        loads[2 + 2 * height].wait()

        def split_proj(step, carry):
            rows = pl.ds(step * 256, 256)
            high, low = split(proj_f[height, rows, :])
            proj_h[height, rows, :] = high
            proj_l[height, rows, :] = low
            return carry

        def split_corr(step, carry):
            rows = pl.ds(step * 32, 32)
            high, low = split(corr_f[height, rows, :])
            corr_h[height, rows, :] = high
            corr_l[height, rows, :] = low
            return carry

        lax.fori_loop(0, half // 256, split_proj, 0)
        lax.fori_loop(0, corr.shape[1] // 32, split_corr, 0)
    loads[1 + 2 * heights].wait()
    loads[2 + 2 * heights].wait()
    tile_rows, slots, tile = near.shape[0], near.shape[1], near.shape[2]

    def split_near(step, carry):
        for slot in range(slots):
            high, low = split(near_f[step, slot])
            near_hl[step, slot * tile:(slot + 1) * tile, :tile] = high
            near_hl[step, slot * tile:(slot + 1) * tile, tile:] = low
        return carry

    lax.fori_loop(0, tile_rows, split_near, 0)

    def split_coup(step, carry):
        high, low = split(coup_f[step])
        coup_h[step] = high
        coup_l[step] = low
        return carry

    lax.fori_loop(0, heights, split_coup, 0)

    for chunk in range(chunks):
        arrivals[chunk].wait_recv()
        place(other, (1 - side) * half, chunk * SRC, False)

    per = POS // tile

    def cut(step, carry):
        for piece in range(per):
            ordered[step * per + piece] = acc[step, :, piece * tile:(piece + 1) * tile].astype(BF16)
        return carry

    lax.fori_loop(0, order.shape[0], cut, 0)

    for row in range(tile_rows):
        picked = []
        for slot in range(slots):
            live = jnp.where(slot < near_count[row], 1.0, 0.0).astype(F32)
            block = ordered[near_index[row, slot]]
            picked.append((block.astype(F32) * live).astype(BF16))
        four = dot(jnp.concatenate(picked, axis=1), near_hl[row])
        current[:, row * tile:(row + 1) * tile] = (
            four[:rhs_count, :tile] + (four[:rhs_count, tile:] + four[rhs_count:, :tile])
            + four[rhs_count:, tile:]
        )

    for height in range(heights):
        got = dot3(stacked(current[...]), proj_h[height], proj_l[height])
        part[height] = got.reshape(part.shape[1:])
        own = sib = None
        if height == 0:
            waits = []
            for rel in range(1, 4):
                there = rank0
                for bit in (1, 2):
                    if rel & bit:
                        there = flip(there, bit)
                waits.append(send(
                    part.at[0, pl.ds(2 * there, 2)], rs0.at[rel],
                    rs_send.at[0, rel], rs_recv.at[0, rel], plane(rel),
                ))
            for wait in waits:
                wait.wait_recv()
            near_sum = part[0, pl.ds(2 * rank0, 2)] + rs0[1]
            far_sum = rs0[2] + rs0[3]
            stage0[0] = near_sum
            stage0[1] = far_sum
            stage0[2] = near_sum
            ag0[rank0, 0] = near_sum
            ag0[rank0, 1] = far_sum
            waits = []
            for rel in range(1, 4):
                first = 1 if rel & 2 else 0
                waits.append(send(
                    stage0.at[pl.ds(first, 2)], ag0.at[rank0],
                    ag_send.at[0, rel], ag_recv.at[0, rel], plane(rel),
                ))
            for wait in waits:
                wait.wait_recv()
            own = ag0[:, 0].reshape(rhs_count, -1)
            sib = ag0[:, 1].reshape(rhs_count, -1)
        else:
            waits = []
            for rel in range(1, 8):
                waits.append(send(
                    part.at[height, rank_of(rel)], rs.at[height, rel],
                    rs_send.at[height, rel], rs_recv.at[height, rel], plane(rel),
                ))
            for wait in waits:
                wait.wait_recv()
            near_sum = (part[height, rank] + rs[height, 1]) + (rs[height, 2] + rs[height, 3])
            far_sum = (rs[height, 4] + rs[height, 5]) + (rs[height, 6] + rs[height, 7])
            swap = height == 1
            if height > 1:
                whole = near_sum + far_sum
                zsend[height] = whole
                waits = []
                for rel in range(1, 2 ** (height - 1)):
                    waits.append(send(
                        zsend.at[height], zrecv.at[height, rel],
                        z_send.at[height, rel], z_recv.at[height, rel], column_of(rel),
                    ))
                for wait in waits:
                    wait.wait_recv()
                if height == 2:
                    near_sum, far_sum = whole, zrecv[height, 1]
                else:
                    near_sum = whole + zrecv[height, 1]
                    far_sum = zrecv[height, 2] + zrecv[height, 3]
            stage[height, 0] = near_sum
            stage[height, 1] = far_sum
            stage[height, 2] = near_sum
            ag[height, rank, 0] = near_sum
            ag[height, rank, 1] = far_sum
            waits = []
            for rel in range(1, 8):
                first = 1 if swap and rel & 4 else 0
                waits.append(send(
                    stage.at[height, pl.ds(first, 2)], ag.at[height, rank],
                    ag_send.at[height, rel], ag_recv.at[height, rel], plane(rel),
                ))
            for wait in waits:
                wait.wait_recv()
            own = ag[height, :, 0].reshape(rhs_count, -1)
            sib = ag[height, :, 1].reshape(rhs_count, -1)
        coeff = dot3(stacked(own), coup_h[height, 0], coup_l[height, 0])
        coeff = coeff + dot3(stacked(sib), coup_h[height, 1], coup_l[height, 1])
        change = dot3(stacked(coeff), corr_h[height], corr_l[height])
        if height < heights - 1:
            current[...] = current[...] - change
        else:
            out[...] = current[...] - change

    for copy in sends:
        copy.wait_send()


def local(
    charges, cluster_order, near_tiles, near_index, near_count, proj_basis, corr_basis, coupling
):
    rhs_count, half = charges.shape
    heights, _, rank = proj_basis.shape
    leaf_size = cluster_order.shape[0]
    tile_rows, slots, tile, _ = near_tiles.shape
    eighth = rhs_count // 8
    any_space = pl.BlockSpec(memory_space=pl.ANY)
    smem = pl.BlockSpec(memory_space=pltpu.SMEM)
    vmem = pl.BlockSpec(memory_space=pltpu.VMEM)
    dma = pltpu.SemaphoreType.DMA
    return pl.pallas_call(
        kernel,
        out_shape=jax.ShapeDtypeStruct((rhs_count, half), F32),
        in_specs=[smem, smem, vmem, any_space, any_space, any_space, any_space, any_space],
        out_specs=vmem,
        scratch_shapes=[
            pltpu.VMEM((rhs_count, half), F32),
            pltpu.VMEM((rhs_count, half), F32),
            pltpu.VMEM((leaf_size // POS, 2 * rhs_count, POS), F32),
            pltpu.VMEM((leaf_size // tile, 2 * rhs_count, tile), BF16),
            pltpu.VMEM((tile_rows, slots, tile, tile), F32),
            pltpu.VMEM((tile_rows, slots * tile, 2 * tile), BF16),
            pltpu.VMEM((heights, half, rank), F32),
            pltpu.VMEM((heights, half, rank), BF16),
            pltpu.VMEM((heights, half, rank), BF16),
            pltpu.VMEM((heights, rank, half), F32),
            pltpu.VMEM((heights, rank, half), BF16),
            pltpu.VMEM((heights, rank, half), BF16),
            pltpu.VMEM((heights, 2, rank, rank), F32),
            pltpu.VMEM((heights, 2, rank, rank), BF16),
            pltpu.VMEM((heights, 2, rank, rank), BF16),
            pltpu.VMEM((rhs_count, half), F32),
            pltpu.VMEM((heights, 8, eighth, rank), F32),
            pltpu.VMEM((4, 2, eighth, rank), F32),
            pltpu.VMEM((3, 2, eighth, rank), F32),
            pltpu.VMEM((4, 2, 2, eighth, rank), F32),
            pltpu.VMEM((heights, 8, eighth, rank), F32),
            pltpu.VMEM((heights, 3, eighth, rank), F32),
            pltpu.VMEM((heights, 8, 2, eighth, rank), F32),
            pltpu.VMEM((heights, eighth, rank), F32),
            pltpu.VMEM((heights, 4, eighth, rank), F32),
            dma((3 + 2 * heights,)),
            dma((half // SRC,)),
            dma((half // SRC,)),
            dma((heights, 8)),
            dma((heights, 8)),
            dma((heights, 8)),
            dma((heights, 8)),
            dma((heights, 4)),
            dma((heights, 4)),
        ],
        compiler_params=pltpu.CompilerParams(
            collective_id=0, has_side_effects=True, vmem_limit_bytes=60 * 2**20
        ),
        name="solve",
    )(
        near_index,
        near_count,
        cluster_order.reshape(leaf_size // POS, 1, POS),
        charges,
        near_tiles,
        proj_basis,
        corr_basis,
        coupling[0],
    )


def solution(mesh):
    return jax.shard_map(
        local,
        mesh=mesh,
        in_specs=(
            P(None, ("level", "leaf", "rhs")),
            P(("level", "leaf")),
            P(("level", "leaf", "rhs"), None, None, None),
            P(("level", "leaf", "rhs"), None),
            P(("level", "leaf", "rhs")),
            P(None, ("level", "leaf", "rhs"), None),
            P(None, None, ("level", "leaf", "rhs")),
            P(("level", "leaf"), None, None, None, None),
        ),
        out_specs=P(None, ("level", "leaf", "rhs")),
        check_vma=False,
    )
```

time: 228 us -> 69.7 us (0.31)
  waiting for transfers between devices: 140 us -> 0 us
  Pallas kernels: 0 us -> 66.2 us
  matrix products: 34.9 us -> 0 us
  local copies, waits for them, and re-layouts: 23.9 us -> 3.23 us
  between operations: 13.3 us -> 0.01 us
  starting transfers between devices: 10.5 us -> 0 us
  other arithmetic: 4.61 us -> 0 us
    psum x4 -> x0, waiting for transfers between devices: 83.4 us -> none  [local(): own_sum = lax.psum(projected, 'rhs')]
    pallas_call x0 -> x1, Pallas kernels: none -> 66.2 us  [local(): pl.pallas_call(kernel, out_shape=jax.ShapeDtypeStruct((rhs_count, half),...]
    all_gather x1 -> x0, waiting for transfers between devices: 35.6 us -> none  [local(): leaf_charges = lax.all_gather(charges, 'rhs', axis=1, tiled=True)]
    dot_general x17 -> x0, matrix products: 34.9 us -> none  [the longest x4 13.7 us: local(): jnp.dot(current, proj_basis[height], precision=lax.Precision.HIGHEST, pre...]
    ppermute x10 -> x0, waiting for transfers between devices: 21.3 us -> none  [from_partner(): return lax.ppermute(block, axis, route)]
    gather x3 -> x0, local copies, waits for them, and re-layouts: 21.3 us -> none  [the longest x1 15.7 us: local(): ordered = jnp.take(leaf_charges, cluster_order, axis=1)]
    ppermute x10 -> x0, starting transfers between devices: 10.2 us -> none  [from_partner(): return lax.ppermute(block, axis, route)]
    add x6 -> x0, other arithmetic: 2.58 us -> none  [local(): own_sum = own_sum + partner_sum(own_sum, bit_pos)]
  transfers between devices with their start and end apart: 15 -> 0, of which waited for: 15 -> 0; matrix products, arithmetic and copies ran while one was open for 1% -> 0% of each run, Pallas kernels for 0% -> 0%
where the time goes in v1:
time: 69.7 us; the launch traced here: 69.4 us
  Pallas kernels  66.2 us (95%)
  local copies, waits for them, and re-layouts  3.23 us (5%)
    pallas_call x1, Pallas kernels, local(): pl.pallas_call(kernel, out_shape=jax.ShapeDtypeStruct((rhs_count, half),...  66.2 us
    unnamed x2, local copies, waits for them, and re-layouts  3.23 us

profile of v1, /device:TPU:0, one launch (start us, length us, event | category | flops | bytes accessed | tf_op | source)
XLA Modules:
  0.0 69.4 jit_solution(12646979610239100249)
XLA Ops:
  0.0 1.4 %copy.9.near_index = s32[16,4]{1,0:T(8,128)} copy(s32[16,4]{0,1:T(4,128)} %param.11) | data formatting | bytes 512 | tf_op args[3]
  1.4 66.2 %solve.1 = f32[64,2048]{1,0:T(8,128)} custom-call(s32[16,4]{1,0:T(8,128)} %copy.9.near_index, s32[16]{0:T(128)} %near_count.1, s32[8,1,512]{2,1,0:T(1,128)} %bitcast.3, f32[64,2048]{1,0:T(8,128)} %charges.1, f32[16,4,128,128]{3,2,1,0:T(8,128)} %near.1, f32[4,2048,256]{2,1,0:T(8,128)} %proj.1, f32[4,256,2048]{2,1,0:T(8,128)} %corr.1, f32[4,2,256,256]{3,2,1,0:T(8,128)} %bitcast.2), custom_call_target="tpu_custom_call" | custom-call | tf_op jit(solution)/shard_map/solve/pallas_call | solution.py:305
  67.6 1.9 %copy.11 = f32[64,2048]{1,0:T(8,128)} copy(f32[64,2048]{1,0:T(8,128)} %solve.1) | data formatting | bytes 1048576

commit v2 on v1

--- a/solution.py
+++ b/solution.py
@@ -39,7 +39,7 @@
 
 def kernel(
     near_index, near_count, order, charges, near, proj, corr, coup, out,
-    mine, other, acc, ordered, near_f, near_hl, proj_f, proj_h, proj_l, corr_f, corr_h, corr_l,
+    mine, other, hot, ordered, near_f, near_hl, proj_f, proj_h, proj_l, corr_f, corr_h, corr_l,
     coup_f, coup_h, coup_l, current, part, rs0, stage0, ag0, rs, stage, ag, zsend, zrecv,
     load_sem, ex_send, ex_recv, rs_send, rs_recv, ag_send, ag_recv, z_send, z_recv,
 ):
@@ -80,7 +80,7 @@
         loads.append(pltpu.make_async_copy(corr.at[height], corr_f.at[height], load_sem.at[2 + 2 * height]))
     loads.append(pltpu.make_async_copy(near, near_f, load_sem.at[1 + 2 * heights]))
     loads.append(pltpu.make_async_copy(coup, coup_f, load_sem.at[2 + 2 * heights]))
-    for load in loads:
+    for load in [loads[0], loads[1 + 2 * heights], loads[1], loads[2 + 2 * heights]] + loads[2:1 + 2 * heights]:
         load.start()
 
     barrier = pltpu.get_barrier_semaphore()
@@ -110,88 +110,103 @@
         ))
 
     rows_of = lax.broadcasted_iota(jnp.int32, (SUB, POS), 0)
-
-    def place(source, first, start, fresh):
-        parts = stacked(source[:, pl.ds(start, SRC)])
+    tile_rows, slots, tile = near.shape[0], near.shape[1], near.shape[2]
+    per = POS // tile
+
+    def place(source, first, start, width, fresh):
+        pieces = width // SUB
+        parts = jnp.concatenate(
+            [stacked(source[:, start + sub * SUB:start + (sub + 1) * SUB]) for sub in range(pieces)], axis=0
+        )
+        rows = 2 * rhs_count
 
         def body(step, carry):
             wanted = order[step]
-            masks = []
-            for sub in range(SRC // SUB):
-                rel = wanted - (first + start + sub * SUB)
-                masks.append(jnp.where(rows_of == rel, 1.0, 0.0).astype(BF16))
-            got = dot(parts, jnp.concatenate(masks, axis=0))
             if fresh:
-                acc[step] = got
+                hot[step] = jnp.where(rows_of == wanted % SUB, 1.0, 0.0).astype(BF16)
+            got = dot(parts, hot[step])
+            block = jnp.broadcast_to(wanted // SUB - (first + start) // SUB, (rows, POS))
+            if fresh:
+                total = jnp.zeros((rows, POS), F32)
             else:
-                acc[step] = acc[step] + got
+                total = jnp.concatenate(
+                    [ordered[step * per + piece].astype(F32) for piece in range(per)], axis=1
+                )
+            for sub in range(pieces):
+                total = jnp.where(block == sub, got[sub * rows:(sub + 1) * rows], total)
+            for piece in range(per):
+                ordered[step * per + piece] = total[:, piece * tile:(piece + 1) * tile].astype(BF16)
             return carry
 
         lax.fori_loop(0, order.shape[0], body, 0)
 
-    loads[0].wait()
-    for chunk in range(chunks):
-        place(mine, side * half, chunk * SRC, chunk == 0)
-
-    for height in range(heights):
+    def prepare_proj(height):
         loads[1 + 2 * height].wait()
-        loads[2 + 2 * height].wait()
-
-        def split_proj(step, carry):
+
+        def body(step, carry):
             rows = pl.ds(step * 256, 256)
             high, low = split(proj_f[height, rows, :])
             proj_h[height, rows, :] = high
             proj_l[height, rows, :] = low
             return carry
 
-        def split_corr(step, carry):
+        lax.fori_loop(0, half // 256, body, 0)
+
+    def prepare_corr(height):
+        loads[2 + 2 * height].wait()
+
+        def body(step, carry):
             rows = pl.ds(step * 32, 32)
             high, low = split(corr_f[height, rows, :])
             corr_h[height, rows, :] = high
             corr_l[height, rows, :] = low
             return carry
 
-        lax.fori_loop(0, half // 256, split_proj, 0)
-        lax.fori_loop(0, corr.shape[1] // 32, split_corr, 0)
-    loads[1 + 2 * heights].wait()
-    loads[2 + 2 * heights].wait()
-    tile_rows, slots, tile = near.shape[0], near.shape[1], near.shape[2]
-
-    def split_near(step, carry):
-        for slot in range(slots):
-            high, low = split(near_f[step, slot])
-            near_hl[step, slot * tile:(slot + 1) * tile, :tile] = high
-            near_hl[step, slot * tile:(slot + 1) * tile, tile:] = low
-        return carry
-
-    lax.fori_loop(0, tile_rows, split_near, 0)
-
-    def split_coup(step, carry):
-        high, low = split(coup_f[step])
-        coup_h[step] = high
-        coup_l[step] = low
-        return carry
-
-    lax.fori_loop(0, heights, split_coup, 0)
-
+        lax.fori_loop(0, corr.shape[1] // 32, body, 0)
+
+    def prepare_near():
+        loads[1 + 2 * heights].wait()
+
+        def body(step, carry):
+            for slot in range(slots):
+                high, low = split(near_f[step, slot])
+                near_hl[step, slot * tile:(slot + 1) * tile, :tile] = high
+                near_hl[step, slot * tile:(slot + 1) * tile, tile:] = low
+            return carry
+
+        lax.fori_loop(0, tile_rows, body, 0)
+
+    def prepare_coup():
+        loads[2 + 2 * heights].wait()
+
+        def body(step, carry):
+            high, low = split(coup_f[step])
+            coup_h[step] = high
+            coup_l[step] = low
+            return carry
+
+        lax.fori_loop(0, heights, body, 0)
+
+    loads[0].wait()
+    place(mine, side * half, 0, half, True)
     for chunk in range(chunks):
+        if chunk == 0:
+            prepare_near()
+        elif chunk == 1:
+            prepare_proj(0)
+            prepare_coup()
+        elif chunk == 2:
+            prepare_corr(0)
+        elif chunk == 3:
+            prepare_proj(1)
         arrivals[chunk].wait_recv()
-        place(other, (1 - side) * half, chunk * SRC, False)
-
-    per = POS // tile
-
-    def cut(step, carry):
-        for piece in range(per):
-            ordered[step * per + piece] = acc[step, :, piece * tile:(piece + 1) * tile].astype(BF16)
-        return carry
-
-    lax.fori_loop(0, order.shape[0], cut, 0)
+        place(other, (1 - side) * half, chunk * SRC, SRC, False)
 
     for row in range(tile_rows):
         picked = []
         for slot in range(slots):
             live = jnp.where(slot < near_count[row], 1.0, 0.0).astype(F32)
-            block = ordered[near_index[row, slot]]
+            block = ordered[near_index[slot, row]]
             picked.append((block.astype(F32) * live).astype(BF16))
         four = dot(jnp.concatenate(picked, axis=1), near_hl[row])
         current[:, row * tile:(row + 1) * tile] = (
@@ -214,6 +229,7 @@
                     part.at[0, pl.ds(2 * there, 2)], rs0.at[rel],
                     rs_send.at[0, rel], rs_recv.at[0, rel], plane(rel),
                 ))
+            prepare_corr(1)
             for wait in waits:
                 wait.wait_recv()
             near_sum = part[0, pl.ds(2 * rank0, 2)] + rs0[1]
@@ -230,6 +246,7 @@
                     stage0.at[pl.ds(first, 2)], ag0.at[rank0],
                     ag_send.at[0, rel], ag_recv.at[0, rel], plane(rel),
                 ))
+            prepare_proj(2)
             for wait in waits:
                 wait.wait_recv()
             own = ag0[:, 0].reshape(rhs_count, -1)
@@ -241,6 +258,8 @@
                     part.at[height, rank_of(rel)], rs.at[height, rel],
                     rs_send.at[height, rel], rs_recv.at[height, rel], plane(rel),
                 ))
+            if height < 3:
+                prepare_corr(height + 1)
             for wait in waits:
                 wait.wait_recv()
             near_sum = (part[height, rank] + rs[height, 1]) + (rs[height, 2] + rs[height, 3])
@@ -274,6 +293,8 @@
                     stage.at[height, pl.ds(first, 2)], ag.at[height, rank],
                     ag_send.at[height, rel], ag_recv.at[height, rel], plane(rel),
                 ))
+            if height == 1:
+                prepare_proj(3)
             for wait in waits:
                 wait.wait_recv()
             own = ag[height, :, 0].reshape(rhs_count, -1)
@@ -310,7 +331,7 @@
         scratch_shapes=[
             pltpu.VMEM((rhs_count, half), F32),
             pltpu.VMEM((rhs_count, half), F32),
-            pltpu.VMEM((leaf_size // POS, 2 * rhs_count, POS), F32),
+            pltpu.VMEM((leaf_size // POS, SUB, POS), BF16),
             pltpu.VMEM((leaf_size // tile, 2 * rhs_count, tile), BF16),
             pltpu.VMEM((tile_rows, slots, tile, tile), F32),
             pltpu.VMEM((tile_rows, slots * tile, 2 * tile), BF16),
@@ -348,7 +369,7 @@
         ),
         name="solve",
     )(
-        near_index,
+        near_index.T,
         near_count,
         cluster_order.reshape(leaf_size // POS, 1, POS),
         charges,

time: 69.7 us -> 63.8 us (0.915)
  Pallas kernels: 66.2 us -> 61.7 us
  local copies, waits for them, and re-layouts: 3.23 us -> 1.87 us
    pallas_call x1, Pallas kernels: 66.2 us -> 61.7 us  [local(): pl.pallas_call(kernel, out_shape=jax.ShapeDtypeStruct((rhs_count, half),...]
    unnamed x2 -> x1, local copies, waits for them, and re-layouts: 3.23 us -> 1.87 us
where the time goes in v2:
time: 63.8 us; the launch traced here: 63.6 us
  Pallas kernels  61.7 us (97%)
  local copies, waits for them, and re-layouts  1.87 us (3%)
    pallas_call x1, Pallas kernels, local(): pl.pallas_call(kernel, out_shape=jax.ShapeDtypeStruct((rhs_count, half),...  61.7 us
    unnamed x1, local copies, waits for them, and re-layouts  1.87 us

profile of v2, /device:TPU:0, one launch (start us, length us, event | category | flops | bytes accessed | tf_op | source)
XLA Modules:
  0.0 63.6 jit_solution(18127820299413376460)
XLA Ops:
  0.0 61.7 %solve.1 = f32[64,2048]{1,0:T(8,128)} custom-call(s32[4,16]{1,0:T(4,128)} %bitcast.5, s32[16]{0:T(128)} %near_count.1, s32[8,1,512]{2,1,0:T(1,128)} %bitcast.4, f32[64,2048]{1,0:T(8,128)} %charges.1, f32[16,4,128,128]{3,2,1,0:T(8,128)} %near.1, f32[4,2048,256]{2,1,0:T(8,128)} %proj.1, f32[4,256,2048]{2,1,0:T(8,128)} %corr.1, f32[4,2,256,256]{3,2,1,0:T(8,128)} %bitcast.3), custom_call_target="tpu_custom_call" | custom-call | tf_op jit(solution)/shard_map/solve/pallas_call | solution.py:326
  61.7 1.9 %copy.10 = f32[64,2048]{1,0:T(8,128)} copy(f32[64,2048]{1,0:T(8,128)} %solve.1) | data formatting | bytes 1048576

commit v3 on v2

--- a/solution.py
+++ b/solution.py
@@ -40,7 +40,7 @@
 def kernel(
     near_index, near_count, order, charges, near, proj, corr, coup, out,
     mine, other, hot, ordered, near_f, near_hl, proj_f, proj_h, proj_l, corr_f, corr_h, corr_l,
-    coup_f, coup_h, coup_l, current, part, rs0, stage0, ag0, rs, stage, ag, zsend, zrecv,
+    coup_f, coup_h, coup_l, gram_h, gram_l, current, cur_hl, coeffs, part, rs0, stage0, ag0, rs, stage, ag, zsend, zrecv,
     load_sem, ex_send, ex_recv, rs_send, rs_recv, ag_send, ag_recv, z_send, z_recv,
 ):
     heights = proj.shape[0]
@@ -57,7 +57,7 @@
                 number = flip(number, bit)
         return number
 
-    def plane(rel):
+    def plane(rel, over=0):
         where, there = leaf, side
         if rel & 1:
             there = 1 - side
@@ -65,7 +65,7 @@
             where = flip(where, 1)
         if rel & 4:
             where = flip(where, 2)
-        return {"level": level, "leaf": where, "rhs": there}
+        return {"level": flip(level, 1) if over else level, "leaf": where, "rhs": there}
 
     def column_of(rel):
         number = level
@@ -88,7 +88,9 @@
         pl.semaphore_signal(barrier, inc=1, device_id=plane(rel), device_id_type=MESH)
     for rel in range(1, 4):
         pl.semaphore_signal(barrier, inc=1, device_id=column_of(rel), device_id_type=MESH)
-    pl.semaphore_wait(barrier, 10)
+    for rel in range(1, 8):
+        pl.semaphore_signal(barrier, inc=1, device_id=plane(rel, 1), device_id_type=MESH)
+    pl.semaphore_wait(barrier, 17)
 
     sends = []
 
@@ -187,6 +189,23 @@
 
         lax.fori_loop(0, heights, body, 0)
 
+    def gram(low, high):
+        left = jnp.concatenate([corr_h[low], corr_l[low]], axis=0)
+        top, bottom = split(dot3(left, proj_h[high], proj_l[high]))
+        gram_h[low, high] = top
+        gram_l[low, high] = bottom
+
+    def project(height):
+        got = dot3(cur_hl[...], proj_h[height], proj_l[height])
+        part[height] = got.reshape(part.shape[1:])
+
+    def lower(low, high):
+        got = dot3(coeffs[low], gram_h[low, high], gram_l[low, high])
+        part[high] = part[high] - got.reshape(part.shape[1:])
+
+    def correct(height):
+        current[...] = current[...] - dot3(coeffs[height], corr_h[height], corr_l[height])
+
     loads[0].wait()
     place(mine, side * half, 0, half, True)
     for chunk in range(chunks):
@@ -197,8 +216,10 @@
             prepare_coup()
         elif chunk == 2:
             prepare_corr(0)
+            prepare_proj(1)
         elif chunk == 3:
-            prepare_proj(1)
+            gram(0, 1)
+            prepare_proj(2)
         arrivals[chunk].wait_recv()
         place(other, (1 - side) * half, chunk * SRC, SRC, False)
 
@@ -214,9 +235,10 @@
             + four[rhs_count:, tile:]
         )
 
+    cur_hl[...] = stacked(current[...])
+    project(0)
+
     for height in range(heights):
-        got = dot3(stacked(current[...]), proj_h[height], proj_l[height])
-        part[height] = got.reshape(part.shape[1:])
         own = sib = None
         if height == 0:
             waits = []
@@ -229,6 +251,7 @@
                     part.at[0, pl.ds(2 * there, 2)], rs0.at[rel],
                     rs_send.at[0, rel], rs_recv.at[0, rel], plane(rel),
                 ))
+            project(1)
             prepare_corr(1)
             for wait in waits:
                 wait.wait_recv()
@@ -246,7 +269,8 @@
                     stage0.at[pl.ds(first, 2)], ag0.at[rank0],
                     ag_send.at[0, rel], ag_recv.at[0, rel], plane(rel),
                 ))
-            prepare_proj(2)
+            project(2)
+            gram(0, 2)
             for wait in waits:
                 wait.wait_recv()
             own = ag0[:, 0].reshape(rhs_count, -1)
@@ -258,54 +282,81 @@
                     part.at[height, rank_of(rel)], rs.at[height, rel],
                     rs_send.at[height, rel], rs_recv.at[height, rel], plane(rel),
                 ))
-            if height < 3:
-                prepare_corr(height + 1)
+            if height == 1:
+                gram(1, 2)
+                lower(0, 2)
+                prepare_proj(3)
+            elif height == 2:
+                gram(1, 3)
+                lower(0, 3)
+                gram(2, 3)
+            else:
+                correct(1)
+                correct(2)
             for wait in waits:
                 wait.wait_recv()
             near_sum = (part[height, rank] + rs[height, 1]) + (rs[height, 2] + rs[height, 3])
             far_sum = (rs[height, 4] + rs[height, 5]) + (rs[height, 6] + rs[height, 7])
             swap = height == 1
-            if height > 1:
+            waits = []
+            if height == 2:
                 whole = near_sum + far_sum
                 zsend[height] = whole
-                waits = []
-                for rel in range(1, 2 ** (height - 1)):
+                ag[height, rank, 0] = whole
+                for rel in range(8):
                     waits.append(send(
-                        zsend.at[height], zrecv.at[height, rel],
-                        z_send.at[height, rel], z_recv.at[height, rel], column_of(rel),
+                        zsend.at[height], ag.at[height, rank, 1],
+                        z_send.at[height, rel], z_recv.at[height, rel], plane(rel, 1),
                     ))
-                for wait in waits:
-                    wait.wait_recv()
-                if height == 2:
-                    near_sum, far_sum = whole, zrecv[height, 1]
-                else:
+                for rel in range(1, 8):
+                    waits.append(send(
+                        zsend.at[height], ag.at[height, rank, 0],
+                        ag_send.at[height, rel], ag_recv.at[height, rel], plane(rel),
+                    ))
+            else:
+                if height == 3:
+                    whole = near_sum + far_sum
+                    zsend[height] = whole
+                    crossings = []
+                    for rel in range(1, 4):
+                        crossings.append(send(
+                            zsend.at[height], zrecv.at[height, rel],
+                            z_send.at[height, rel], z_recv.at[height, rel], column_of(rel),
+                        ))
+                    for wait in crossings:
+                        wait.wait_recv()
                     near_sum = whole + zrecv[height, 1]
                     far_sum = zrecv[height, 2] + zrecv[height, 3]
-            stage[height, 0] = near_sum
-            stage[height, 1] = far_sum
-            stage[height, 2] = near_sum
-            ag[height, rank, 0] = near_sum
-            ag[height, rank, 1] = far_sum
-            waits = []
-            for rel in range(1, 8):
-                first = 1 if swap and rel & 4 else 0
-                waits.append(send(
-                    stage.at[height, pl.ds(first, 2)], ag.at[height, rank],
-                    ag_send.at[height, rel], ag_recv.at[height, rel], plane(rel),
-                ))
+                stage[height, 0] = near_sum
+                stage[height, 1] = far_sum
+                stage[height, 2] = near_sum
+                ag[height, rank, 0] = near_sum
+                ag[height, rank, 1] = far_sum
+                for rel in range(1, 8):
+                    first = 1 if swap and rel & 4 else 0
+                    waits.append(send(
+                        stage.at[height, pl.ds(first, 2)], ag.at[height, rank],
+                        ag_send.at[height, rel], ag_recv.at[height, rel], plane(rel),
+                    ))
             if height == 1:
-                prepare_proj(3)
+                project(3)
+                prepare_corr(2)
+                gram(0, 3)
+            elif height == 2:
+                lower(1, 3)
+                prepare_corr(3)
+                correct(0)
             for wait in waits:
                 wait.wait_recv()
             own = ag[height, :, 0].reshape(rhs_count, -1)
             sib = ag[height, :, 1].reshape(rhs_count, -1)
         coeff = dot3(stacked(own), coup_h[height, 0], coup_l[height, 0])
         coeff = coeff + dot3(stacked(sib), coup_h[height, 1], coup_l[height, 1])
-        change = dot3(stacked(coeff), corr_h[height], corr_l[height])
+        coeffs[height] = stacked(coeff)
         if height < heights - 1:
-            current[...] = current[...] - change
+            lower(height, height + 1)
         else:
-            out[...] = current[...] - change
+            out[...] = current[...] - dot3(coeffs[height], corr_h[height], corr_l[height])
 
     for copy in sends:
         copy.wait_send()
@@ -344,7 +395,11 @@
             pltpu.VMEM((heights, 2, rank, rank), F32),
             pltpu.VMEM((heights, 2, rank, rank), BF16),
             pltpu.VMEM((heights, 2, rank, rank), BF16),
+            pltpu.VMEM((heights, heights, rank, rank), BF16),
+            pltpu.VMEM((heights, heights, rank, rank), BF16),
             pltpu.VMEM((rhs_count, half), F32),
+            pltpu.VMEM((2 * rhs_count, half), BF16),
+            pltpu.VMEM((heights, 2 * rhs_count, rank), BF16),
             pltpu.VMEM((heights, 8, eighth, rank), F32),
             pltpu.VMEM((4, 2, eighth, rank), F32),
             pltpu.VMEM((3, 2, eighth, rank), F32),
@@ -361,8 +416,8 @@
             dma((heights, 8)),
             dma((heights, 8)),
             dma((heights, 8)),
-            dma((heights, 4)),
-            dma((heights, 4)),
+            dma((heights, 8)),
+            dma((heights, 8)),
         ],
         compiler_params=pltpu.CompilerParams(
             collective_id=0, has_side_effects=True, vmem_limit_bytes=60 * 2**20

time: 63.8 us -> 61 us (0.956)
  Pallas kernels: 61.7 us -> 58.9 us
    pallas_call x1, Pallas kernels: 61.7 us -> 58.9 us  [local(): pl.pallas_call(kernel, out_shape=jax.ShapeDtypeStruct((rhs_count, half),...]
where the time goes in v3:
time: 61 us; the launch traced here: 60.8 us
  Pallas kernels  58.9 us (97%)
  local copies, waits for them, and re-layouts  1.87 us (3%)
    pallas_call x1, Pallas kernels, local(): pl.pallas_call(kernel, out_shape=jax.ShapeDtypeStruct((rhs_count, half),...  58.9 us
    unnamed x1, local copies, waits for them, and re-layouts  1.87 us

profile of v3, /device:TPU:0, one launch (start us, length us, event | category | flops | bytes accessed | tf_op | source)
XLA Modules:
  0.0 60.8 jit_solution(10113337393934131936)
XLA Ops:
  0.0 58.9 %solve.1 = f32[64,2048]{1,0:T(8,128)} custom-call(s32[4,16]{1,0:T(4,128)} %bitcast.5, s32[16]{0:T(128)} %near_count.1, s32[8,1,512]{2,1,0:T(1,128)} %bitcast.4, f32[64,2048]{1,0:T(8,128)} %charges.1, f32[16,4,128,128]{3,2,1,0:T(8,128)} %near.1, f32[4,2048,256]{2,1,0:T(8,128)} %proj.1, f32[4,256,2048]{2,1,0:T(8,128)} %corr.1, f32[4,2,256,256]{3,2,1,0:T(8,128)} %bitcast.3), custom_call_target="tpu_custom_call" | custom-call | tf_op jit(solution)/shard_map/solve/pallas_call | solution.py:377
  58.9 1.9 %copy.10 = f32[64,2048]{1,0:T(8,128)} copy(f32[64,2048]{1,0:T(8,128)} %solve.1) | data formatting | bytes 1048576

commit v4 on v3

--- a/solution.py
+++ b/solution.py
@@ -80,7 +80,7 @@
         loads.append(pltpu.make_async_copy(corr.at[height], corr_f.at[height], load_sem.at[2 + 2 * height]))
     loads.append(pltpu.make_async_copy(near, near_f, load_sem.at[1 + 2 * heights]))
     loads.append(pltpu.make_async_copy(coup, coup_f, load_sem.at[2 + 2 * heights]))
-    for load in [loads[0], loads[1 + 2 * heights], loads[1], loads[2 + 2 * heights]] + loads[2:1 + 2 * heights]:
+    for load in [loads[0], loads[1 + 2 * heights], loads[1]]:
         load.start()
 
     barrier = pltpu.get_barrier_semaphore()
@@ -110,6 +110,9 @@
         arrivals.append(send(
             charges.at[:, cols], other.at[:, cols], ex_send.at[chunk], ex_recv.at[chunk], plane(1)
         ))
+
+    for load in [loads[2 + 2 * heights]] + loads[2:1 + 2 * heights]:
+        load.start()
 
     rows_of = lax.broadcasted_iota(jnp.int32, (SUB, POS), 0)
     tile_rows, slots, tile = near.shape[0], near.shape[1], near.shape[2]
@@ -192,19 +195,22 @@
     def gram(low, high):
         left = jnp.concatenate([corr_h[low], corr_l[low]], axis=0)
         top, bottom = split(dot3(left, proj_h[high], proj_l[high]))
-        gram_h[low, high] = top
-        gram_l[low, high] = bottom
+        gram_h[low] = top
+        gram_l[low] = bottom
 
     def project(height):
         got = dot3(cur_hl[...], proj_h[height], proj_l[height])
         part[height] = got.reshape(part.shape[1:])
 
     def lower(low, high):
-        got = dot3(coeffs[low], gram_h[low, high], gram_l[low, high])
+        got = dot3(coeffs[low], gram_h[low], gram_l[low])
         part[high] = part[high] - got.reshape(part.shape[1:])
 
     def correct(height):
-        current[...] = current[...] - dot3(coeffs[height], corr_h[height], corr_l[height])
+        left = current[...] - dot3(coeffs[height], corr_h[height], corr_l[height])
+        current[...] = left
+        if height < heights - 2:
+            cur_hl[...] = stacked(left)
 
     loads[0].wait()
     place(mine, side * half, 0, half, True)
@@ -269,8 +275,7 @@
                     stage0.at[pl.ds(first, 2)], ag0.at[rank0],
                     ag_send.at[0, rel], ag_recv.at[0, rel], plane(rel),
                 ))
-            project(2)
-            gram(0, 2)
+            gram(1, 2)
             for wait in waits:
                 wait.wait_recv()
             own = ag0[:, 0].reshape(rhs_count, -1)
@@ -283,15 +288,12 @@
                     rs_send.at[height, rel], rs_recv.at[height, rel], plane(rel),
                 ))
             if height == 1:
-                gram(1, 2)
-                lower(0, 2)
+                correct(0)
                 prepare_proj(3)
             elif height == 2:
-                gram(1, 3)
-                lower(0, 3)
+                correct(1)
                 gram(2, 3)
             else:
-                correct(1)
                 correct(2)
             for wait in waits:
                 wait.wait_recv()
@@ -339,13 +341,11 @@
                         ag_send.at[height, rel], ag_recv.at[height, rel], plane(rel),
                     ))
             if height == 1:
+                project(2)
+                prepare_corr(2)
+            elif height == 2:
                 project(3)
-                prepare_corr(2)
-                gram(0, 3)
-            elif height == 2:
-                lower(1, 3)
                 prepare_corr(3)
-                correct(0)
             for wait in waits:
                 wait.wait_recv()
             own = ag[height, :, 0].reshape(rhs_count, -1)
@@ -395,8 +395,8 @@
             pltpu.VMEM((heights, 2, rank, rank), F32),
             pltpu.VMEM((heights, 2, rank, rank), BF16),
             pltpu.VMEM((heights, 2, rank, rank), BF16),
-            pltpu.VMEM((heights, heights, rank, rank), BF16),
-            pltpu.VMEM((heights, heights, rank, rank), BF16),
+            pltpu.VMEM((heights, rank, rank), BF16),
+            pltpu.VMEM((heights, rank, rank), BF16),
             pltpu.VMEM((rhs_count, half), F32),
             pltpu.VMEM((2 * rhs_count, half), BF16),
             pltpu.VMEM((heights, 2 * rhs_count, rank), BF16),

time: 61 us -> 60.9 us (level)
  no operation moved by 1% of the time
where the time goes in v4:
time: 60.9 us; the launch traced here: 60.7 us
  Pallas kernels  58.8 us (97%)
  local copies, waits for them, and re-layouts  1.87 us (3%)
    pallas_call x1, Pallas kernels, local(): pl.pallas_call(kernel, out_shape=jax.ShapeDtypeStruct((rhs_count, half),...  58.8 us
    unnamed x1, local copies, waits for them, and re-layouts  1.87 us

profile of v4, /device:TPU:0, one launch (start us, length us, event | category | flops | bytes accessed | tf_op | source)
XLA Modules:
  0.0 60.7 jit_solution(9501957587940659013)
XLA Ops:
  0.0 58.8 %solve.1 = f32[64,2048]{1,0:T(8,128)} custom-call(s32[4,16]{1,0:T(4,128)} %bitcast.5, s32[16]{0:T(128)} %near_count.1, s32[8,1,512]{2,1,0:T(1,128)} %bitcast.4, f32[64,2048]{1,0:T(8,128)} %charges.1, f32[16,4,128,128]{3,2,1,0:T(8,128)} %near.1, f32[4,2048,256]{2,1,0:T(8,128)} %proj.1, f32[4,256,2048]{2,1,0:T(8,128)} %corr.1, f32[4,2,256,256]{3,2,1,0:T(8,128)} %bitcast.3), custom_call_target="tpu_custom_call" | custom-call | tf_op jit(solution)/shard_map/solve/pallas_call | solution.py:377
  58.8 1.9 %copy.10 = f32[64,2048]{1,0:T(8,128)} copy(f32[64,2048]{1,0:T(8,128)} %solve.1) | data formatting | bytes 1048576
